TPU v7x, 32 devices: a whole 2x2x4 slice. The times are simulated.
32 devices in a mesh: dp: 8 (over y, x, core), tensor: 4 (over z).
Axes of the slice: x: 2, y: 2, z: 4, core: 2. Of those that a mesh axis runs over, the one named last changes fastest.
Arguments:
- tokens: bfloat16 [8, 512, 1024], P('dp'), may hold values from -6 to 6
- segment_ids: int32 [8, 512], P('dp'), may hold values from 0 to 9, never falling along the last dimension, each value on 1 to 200 neighbouring positions
- cotangent: bfloat16 [8, 512, 1024], P('dp'), may hold values from -6 to 6
- qkv_weight: bfloat16 [2, 1024, 3, 1024], P(None, None, None, 'tensor'), may hold values from -0.1875 to 0.1875
- qv_bias: bfloat16 [2, 2, 1024], P(None, None, 'tensor'), may hold values from -3 to 3
- proj_weight: bfloat16 [2, 1024, 1024], P(None, 'tensor'), may hold values from -1 to 1
- proj_bias: bfloat16 [2, 1024], replicated, may hold values from -2 to 2
- first_gain: bfloat16 [2, 1024], replicated, may hold values from 0.099609375 to 1.8984375
- first_shift: bfloat16 [2, 1024], replicated, may hold values from -2 to 2
- up_weight: bfloat16 [2, 1024, 4096], P(None, None, 'tensor'), may hold values from -0.1875 to 0.1875
- up_bias: bfloat16 [2, 4096], P(None, 'tensor'), may hold values from -3 to 3
- down_weight: bfloat16 [2, 4096, 1024], P(None, 'tensor'), may hold values from -0.09375 to 0.09375
- down_bias: bfloat16 [2, 1024], replicated, may hold values from -2 to 2
- second_gain: bfloat16 [2, 1024], replicated, may hold values from 0.099609375 to 1.8984375
- second_shift: bfloat16 [2, 1024], replicated, may hold values from -2 to 2
Outputs:
- mixed: float32 [8, 512, 1024], P('dp')
- input_grad: float32 [8, 512, 1024], P('dp')
- qkv_weight_grad: float32 [2, 1024, 3, 1024], P(None, None, None, 'tensor')
- qv_bias_grad: float32 [2, 2, 1024], P(None, None, 'tensor')
- proj_weight_grad: float32 [2, 1024, 1024], P(None, 'tensor')
- proj_bias_grad: float32 [2, 1024], replicated
- first_gain_grad: float32 [2, 1024], replicated
- first_shift_grad: float32 [2, 1024], replicated
- up_weight_grad: float32 [2, 1024, 4096], P(None, None, 'tensor')
- up_bias_grad: float32 [2, 4096], P(None, 'tensor')
- down_weight_grad: float32 [2, 4096, 1024], P(None, 'tensor')
- down_bias_grad: float32 [2, 1024], replicated
- second_gain_grad: float32 [2, 1024], replicated
- second_shift_grad: float32 [2, 1024], replicated
Inputs may be any that keep to these rules, and one draw needn't show every extreme that they name: `segment_ids`: within a sequence the document number never falls; every document holds 1 to 200 tokens, and tokens attend only within their document.
All inputs are finite; a program needn't handle non-finite values.
Results may differ from a plain program's by a relative error of at most 0.034.
Values may be sent and summed in bfloat16 or wider, within the bound.
A program may use at most 192 MiB of HBM per device.

v0:
```python
import math
import types

import jax
import jax.numpy as jnp
from jax import lax
from jax.experimental import pallas as pl
from jax.experimental.pallas import tpu as pltpu
from jax.sharding import PartitionSpec as P

HEAD = 64


norm_eps = 1e-12
masked_value = -1000000000.0


MESH = pl.DeviceIdType.MESH
F32 = jnp.float32
LOW = jnp.bfloat16
CHUNK = 32
LAG = 2
PIECE = 512
QUERIES = 128


def dot(a, b):
    return jnp.dot(a, b, preferred_element_type=F32)


def dot_t(a, b):
    return lax.dot_general(a, b, (((1,), (1,)), ((), ())), preferred_element_type=F32)


def dot_tn(a, b):
    return lax.dot_general(a, b, (((0,), (0,)), ((), ())), preferred_element_type=F32)


def here():
    return lax.axis_index("dp"), lax.axis_index("tensor")


def greet(size, line=True, targets=()):
    row, place = here()
    barrier = pltpu.get_barrier_semaphore()
    for count, target in targets:

        def signal(index, carry):
            pl.semaphore_signal(barrier, inc=1, device_id=target(index), device_id_type=MESH)
            return carry

        lax.fori_loop(0, count, signal, 0)
    expected = sum(count for count, _ in targets)
    left, right = place > 0, place < size - 1
    if line:

        @pl.when(left)
        def _():
            pl.semaphore_signal(barrier, inc=1, device_id=(row, place - 1), device_id_type=MESH)

        @pl.when(right)
        def _():
            pl.semaphore_signal(barrier, inc=1, device_id=(row, place + 1), device_id_type=MESH)

    def wait():
        if not line:
            pl.semaphore_wait(barrier, expected)
            return

        @pl.when(left & right)
        def _():
            pl.semaphore_wait(barrier, expected + 2)

        @pl.when(jnp.logical_not(left & right))
        def _():
            pl.semaphore_wait(barrier, expected + 1)

    return wait


def partner():
    row, place = here()
    return (row + 1 - 2 * lax.rem(row, 2), place)


def line_loop(size, stages, extras=(), lag=LAG):
    row, place = here()
    half = stages[0].part.shape[0] // 2
    chunks = half // CHUNK
    end = size - 1
    span = 2 * lag * end

    def rows_of(side, chunk):
        return pl.ds(pl.multiple_of(side * half + chunk * CHUNK, CHUNK), CHUNK)

    def sum_copy(stage, side, chunk, target):
        rows = rows_of(side, chunk)
        return pltpu.make_async_remote_copy(
            src_ref=stage.part.at[rows],
            dst_ref=stage.recv.at[rows],
            send_sem=stage.sems[0].at[side, chunk],
            recv_sem=stage.sems[1].at[side, chunk],
            device_id=(row, target),
            device_id_type=MESH,
        )

    def row_copy(stage, which, side, chunk, target):
        rows = rows_of(side, chunk)
        return pltpu.make_async_remote_copy(
            src_ref=stage.outs[which].at[rows],
            dst_ref=stage.outs[which].at[rows],
            send_sem=stage.sems[2].at[which, side, chunk],
            recv_sem=stage.sems[3].at[which, side, chunk],
            device_id=(row, target),
            device_id_type=MESH,
        )

    def side_facts(side):
        if side == 0:
            return place, place + 1, place - 1
        return end - place, place - 1, place + 1

    def bring_back(stage, since):
        for side in range(2):
            at, onward, back = side_facts(side)
            chunk = since - lag * end - lag * (end - at)

            @pl.when((at < end) & (chunk >= 0) & (chunk < chunks))
            def _():
                for which in range(len(stage.outs)):
                    row_copy(stage, which, side, chunk, back).wait_recv()

                    @pl.when(at > 0)
                    def _():
                        row_copy(stage, which, side, chunk, back).start()

    def sum_up(stage, since):
        for side in range(2):
            at, onward, back = side_facts(side)
            chunk = since - lag * at

            @pl.when((chunk >= 0) & (chunk < chunks))
            def _():
                @pl.when(at > 0)
                def _():
                    sum_copy(stage, side, chunk, onward).wait_recv()

                @pl.when(at < end)
                def _():
                    @pl.when(at > 0)
                    def _():
                        rows = rows_of(side, chunk)
                        total = stage.part[rows].astype(F32) + stage.recv[rows].astype(F32)
                        stage.part[rows] = total.astype(LOW)

                    sum_copy(stage, side, chunk, onward).start()

                @pl.when(at == end)
                def _():
                    rows = rows_of(side, chunk)
                    own = pl.ds(pl.multiple_of(chunk * CHUNK, CHUNK), CHUNK)
                    stage.finish(rows, own, stage.part[rows].astype(F32) + stage.recv[rows].astype(F32))
                    for which in range(len(stage.outs)):
                        row_copy(stage, which, side, chunk, back).start()

    def step(now, carry):
        for number, stage in enumerate(stages):
            bring_back(stage, now - number * span)
        for number, stage in enumerate(stages):
            since = now - number * span

            @pl.when((since >= 0) & (since < chunks))
            def _():
                stage.produce([rows_of(side, since) for side in range(2)])

            sum_up(stage, since)
        for first, count, work in extras:

            @pl.when((now >= first) & (now < first + count))
            def _():
                work(now - first)

        return carry

    lax.fori_loop(0, chunks + span * len(stages), step, 0)

    def drain(chunk, carry):
        for stage in stages:
            for side in range(2):
                at, onward, back = side_facts(side)

                @pl.when(at < end)
                def _():
                    sum_copy(stage, side, chunk, onward).wait_send()

                @pl.when(at > 0)
                def _():
                    for which in range(len(stage.outs)):
                        row_copy(stage, which, side, chunk, back).wait_send()

        return carry

    lax.fori_loop(0, chunks, drain, 0)


def by_rows(count, work, block=32):
    def one(index, carry):
        work(pl.ds(pl.multiple_of(index * block, block), block), index * block)
        return carry

    block = min(block, count)
    lax.fori_loop(0, count // block, one, 0)


class Spread:
    def __init__(self, chips, grads, scratch):
        self.chips, self.grads = chips, grads
        self.half = grads.shape[0] // 2
        self.near, self.far, self.near_sems, self.far_sems, self.free = scratch
        row, place = here()
        self.core, self.chip, self.place = lax.rem(row, 2), row // 2, place

    @staticmethod
    def scratch(chips, rows, width):
        half = rows // 2
        far = half * 3 // 4 if chips == 4 else half // chips * (chips - 1)
        copies = 8 if chips == 4 else 2 * (chips - 1)
        sems = [
            pltpu.SemaphoreType.DMA((4,)),
            pltpu.SemaphoreType.DMA((2, copies)),
            pltpu.SemaphoreType.REGULAR,
        ]
        return [pltpu.VMEM((half, width), LOW), pltpu.VMEM((far, width), LOW), *sems, *sems]

    def rows(self, first, count):
        return pl.ds(pl.multiple_of(first, 16), count)

    def core_copy(self, source, target, number):
        return pltpu.make_async_remote_copy(
            src_ref=source,
            dst_ref=target,
            send_sem=self.near_sems.at[2 * number],
            recv_sem=self.near_sems.at[2 * number + 1],
            device_id=partner(),
            device_id_type=MESH,
        )

    def near_copy(self):
        other = self.rows((1 - self.core) * self.half, self.half)
        return self.core_copy(self.grads.at[other], self.near, 0)

    def last_copy(self):
        own = self.grads.at[self.rows(self.core * self.half, self.half)]
        return self.core_copy(own, own, 1)

    def chip_copy(self, source, target, number, chip):
        return pltpu.make_async_remote_copy(
            src_ref=source,
            dst_ref=target,
            send_sem=self.far_sems.at[0, number],
            recv_sem=self.far_sems.at[1, number],
            device_id=(chip * 2 + self.core, self.place),
            device_id_type=MESH,
        )

    def to_partner(self):
        self.near_copy().start()

    def add_partner(self):
        self.near_copy().wait_send()
        pl.semaphore_signal(self.free, inc=1, device_id=partner(), device_id_type=MESH)
        self.near_copy().wait_recv()
        base = self.core * self.half

        def add(rows, first):
            own = self.grads[self.rows(base + first, rows.size)]
            self.near[rows] = self.near[rows] + own

        by_rows(self.half, add)

    def to_other_core(self):
        self.take_back()
        self.settle_chips()
        pl.semaphore_wait(self.free, 1)
        self.last_copy().start()

    def settle(self):
        self.last_copy().wait_recv()
        self.last_copy().wait_send()


class DirectSpread(Spread):
    def each(self, work):
        def one(index, carry):
            work(index)
            return carry

        lax.fori_loop(0, self.chips - 1, one, 0)

    def peer(self, index):
        return lax.rem(self.chip + index + 1, self.chips)

    def far_copy(self, index):
        count = self.half // self.chips
        chip = self.peer(index)
        source = self.near.at[self.rows(chip * count, count)]
        return self.chip_copy(source, self.far.at[self.rows(index * count, count)], index, chip)

    def back_copy(self, index):
        count = self.half // self.chips
        share = self.grads.at[self.rows(self.core * self.half + self.chip * count, count)]
        return self.chip_copy(share, share, self.chips - 1 + index, self.peer(index))

    def to_chips(self):
        self.add_partner()
        self.each(lambda index: self.far_copy(index).start())

    def onward(self):
        pass

    def give_share(self):
        self.each(lambda index: self.far_copy(index).wait_recv())
        count = self.half // self.chips
        base = self.chip * count

        def add(rows, first):
            def one(index, total):
                return total + self.far[self.rows(index * count + first, rows.size)].astype(F32)

            own = self.near[self.rows(base + first, rows.size)].astype(F32)
            total = lax.fori_loop(0, self.chips - 1, one, own)
            self.grads[self.rows(self.core * self.half + base + first, rows.size)] = total.astype(LOW)

        by_rows(count, add)
        self.each(lambda index: self.back_copy(index).start())

    def pass_on(self):
        pass

    def take_back(self):
        self.each(lambda index: self.back_copy(index).wait_recv())

    def settle_chips(self):
        self.each(lambda index: self.far_copy(index).wait_send())
        self.each(lambda index: self.back_copy(index).wait_send())


class SquareSpread(Spread):
    def __init__(self, chips, grads, scratch):
        super().__init__(chips, grads, scratch)
        quarter = self.half // 4
        eighth = self.half // 8
        first, second = lax.rem(self.chip, 2), self.chip // 2
        along = self.chip + 1 - 2 * first
        across = self.chip + 2 - 4 * second
        self.quarter, self.eighth = quarter, eighth
        self.chips_of = ((along, across), (across, along))
        self.bits = ((first, second), (second, first))
        self.part = [side * 2 * quarter for side in range(2)]
        self.kept = [self.part[side] + self.bits[side][0] * quarter for side in range(2)]
        self.own = [self.kept[side] + self.bits[side][1] * eighth for side in range(2)]

    def first_copy(self, side):
        sent = self.part[side] + (1 - self.bits[side][0]) * self.quarter
        room = self.far.at[pl.ds(side * self.quarter, self.quarter)]
        source = self.near.at[self.rows(sent, self.quarter)]
        return self.chip_copy(source, room, side, self.chips_of[side][0])

    def second_copy(self, side):
        sent = self.kept[side] + (1 - self.bits[side][1]) * self.eighth
        room = self.far.at[pl.ds(2 * self.quarter + side * self.eighth, self.eighth)]
        source = self.near.at[self.rows(sent, self.eighth)]
        return self.chip_copy(source, room, 2 + side, self.chips_of[side][1])

    def share_copy(self, side):
        share = self.grads.at[self.rows(self.core * self.half + self.own[side], self.eighth)]
        return self.chip_copy(share, share, 4 + side, self.chips_of[side][1])

    def pass_copy(self, side):
        share = self.grads.at[self.rows(self.core * self.half + self.kept[side], self.quarter)]
        return self.chip_copy(share, share, 6 + side, self.chips_of[side][0])

    def to_chips(self):
        self.add_partner()
        for side in range(2):
            self.first_copy(side).start()

    def onward(self):
        for side in range(2):
            self.first_copy(side).wait_recv()
            base = self.kept[side]

            def add(rows, first, side=side, base=base):
                at = self.rows(base + first, rows.size)
                came = self.far[self.rows(side * self.quarter + first, rows.size)]
                self.near[at] = self.near[at] + came

            by_rows(self.quarter, add)
            self.second_copy(side).start()

    def give_share(self):
        for side in range(2):
            self.second_copy(side).wait_recv()
            base = self.own[side]

            def add(rows, first, side=side, base=base):
                came = self.far[self.rows(2 * self.quarter + side * self.eighth + first, rows.size)]
                total = self.near[self.rows(base + first, rows.size)].astype(F32) + came.astype(F32)
                to = self.rows(self.core * self.half + base + first, rows.size)
                self.grads[to] = total.astype(LOW)

            by_rows(self.eighth, add)
            self.share_copy(side).start()

    def pass_on(self):
        for side in range(2):
            self.share_copy(side).wait_recv()
            self.pass_copy(side).start()

    def take_back(self):
        for side in range(2):
            self.pass_copy(side).wait_recv()

    def settle_chips(self):
        for side in range(2):
            self.first_copy(side).wait_send()
            self.second_copy(side).wait_send()
            self.share_copy(side).wait_send()
            self.pass_copy(side).wait_send()


def spread_of(chips, grads, scratch):
    return (SquareSpread if chips == 4 else DirectSpread)(chips, grads, scratch)


def normalize(residual):
    centred = residual - jnp.mean(residual, axis=-1, keepdims=True)
    inverse = lax.rsqrt(jnp.mean(centred * centred, axis=-1, keepdims=True) + norm_eps)
    return centred * inverse, inverse


def norm_back(grad, gain, unit, inverse):
    scaled = grad * gain
    return (
        scaled
        - jnp.mean(scaled, axis=-1, keepdims=True)
        - unit * jnp.mean(scaled * unit, axis=-1, keepdims=True)
    ) * inverse


def tally(total, values):
    total[...] += jnp.sum(values.reshape(-1, 8, values.shape[-1]), axis=0)


class Layer:
    def __init__(self, array, layer):
        self.array, self.layer = array, layer

    def room(self):
        return self.array.shape if self.layer is None else self.array.shape[1:]


def whole(array):
    return Layer(array, None)


def view(refs, suffix):
    named = dict(vars(refs))
    for name, ref in vars(refs).items():
        if name.endswith(suffix):
            named[name[: -len(suffix)]] = ref
    return types.SimpleNamespace(**named)


def call(collective, body, ins, outs, scratch, into=types.MappingProxyType({}), later=(), sent=()):
    vmem = pl.BlockSpec(memory_space=pltpu.VMEM)
    names = [*ins, *outs]
    fetched = {name: value for name, value in ins.items() if isinstance(value, Layer)}
    inside = {name: value for name, value in fetched.items() if name not in into}
    extra = {name: spec if isinstance(spec, list) else [spec] for name, spec in scratch.items()}

    def run(*refs):
        named = dict(zip(names, refs))
        rest = list(refs[len(names) :])
        copies, leaving = {}, {}
        arrivals, departures = rest.pop(0), rest.pop(0)
        for number, name in enumerate(sent):
            room = rest.pop(0)
            leaving[name] = pltpu.make_async_copy(room, named[name], departures.at[number])
            named[name] = room
        for number, (name, value) in enumerate(fetched.items()):
            room = named[into[name]] if name in into else rest.pop(0)
            source = named[name] if value.layer is None else named[name].at[value.layer]
            copies[name] = pltpu.make_async_copy(source, room, arrivals.at[number])
            if name not in later:
                copies[name].start()
            named[name] = room
        for name, specs in extra.items():
            taken = [rest.pop(0) for _ in specs]
            named[name] = taken if isinstance(scratch[name], list) else taken[0]

        def need(*wanted):
            for name in wanted:
                copies[name].wait()

        def fetch(*wanted):
            for name in wanted:
                copies[name].start()

        def send(*wanted):
            for name in wanted:
                leaving[name].start()

        body(types.SimpleNamespace(**named, need=need, fetch=fetch, send=send))
        for copy in leaving.values():
            copy.wait()

    results = pl.pallas_call(
        run,
        out_shape=list(outs.values()),
        in_specs=[pl.BlockSpec(memory_space=pl.ANY) if name in fetched else vmem for name in ins],
        out_specs=[pl.BlockSpec(memory_space=pl.ANY) if name in sent else vmem for name in outs],
        scratch_shapes=[
            pltpu.SemaphoreType.DMA((len(fetched),)),
            pltpu.SemaphoreType.DMA((max(1, len(sent)),)),
            *(pltpu.VMEM(outs[name].shape, outs[name].dtype) for name in sent),
            *(pltpu.VMEM(value.room(), value.array.dtype) for value in inside.values()),
            *(spec for specs in extra.values() for spec in specs),
        ],
        compiler_params=pltpu.CompilerParams(
            collective_id=collective, has_side_effects=True, vmem_limit_bytes=60 << 20
        ),
    )(*(value.array if isinstance(value, Layer) else value for value in ins.values()))
    return types.SimpleNamespace(**dict(zip(outs, results)))


def shape(*dims, kind=F32):
    return jax.ShapeDtypeStruct(dims, kind)


def line_scratch(rows, width, outs=1):
    chunks = rows // 2 // CHUNK
    return [
        pltpu.VMEM((rows, width), LOW),
        pltpu.VMEM((rows, width), LOW),
        pltpu.SemaphoreType.DMA((2, chunks)),
        pltpu.SemaphoreType.DMA((2, chunks)),
        pltpu.SemaphoreType.DMA((outs, 2, chunks)),
        pltpu.SemaphoreType.DMA((outs, 2, chunks)),
    ]


def stage_of(produce, finish, outs, scratch):
    part, recv, *sems = scratch
    return types.SimpleNamespace(
        produce=produce, finish=finish, outs=outs, part=part, recv=recv, sems=sems
    )


def clear(*refs):
    for ref in refs:
        ref[...] = jnp.zeros_like(ref)


def vector(ref, layer):
    return ref[...].astype(F32)[layer : layer + 1]


def head_lanes(values, head):
    lane = lax.broadcasted_iota(jnp.int32, values.shape, 1)
    return jnp.where(lane // HEAD == head, values, jnp.zeros_like(values))


def turned(values):
    return jnp.transpose(values.astype(F32)).astype(LOW)


def mark_segments(r):
    length = r.seg_row.shape[1]
    wide = jnp.broadcast_to(r.seg_row[...].astype(F32), (QUERIES, length))
    r.seg_cols[...] = jnp.transpose(wide)


def masked_block(r, keys, queries, at):
    same = r.seg_cols[...] == r.seg_row[:, at].astype(F32)
    return jnp.where(same, dot_t(keys, queries) * HEAD ** (-0.5), masked_value)


def project(r, layer):
    bias = r.qv_bias[layer].astype(F32)
    for member in range(3):
        rows = dot(r.low_in[...], r.qkv_w[member])
        if member != 1:
            rows += bias[member // 2 : member // 2 + 1]
        r.projected[member] = rows.astype(LOW)
    r.turned_rows[...] = turned(r.projected[2])


def attend(r, block):
    at = pl.ds(pl.multiple_of(block * QUERIES, QUERIES), QUERIES)
    queries = r.projected[0, at]
    heads = queries.shape[1] // HEAD
    parts = []
    for head in range(heads):
        scores = masked_block(r, r.projected[1], head_lanes(queries, head), at)
        row_max = jnp.max(scores, axis=0, keepdims=True)
        exponent = jnp.exp(scores - row_max)
        row_total = jnp.sum(exponent, axis=0, keepdims=True)
        r.log_total[head : head + 1, at] = row_max + jnp.log(row_total)
        probs = (exponent * (1.0 / row_total)).astype(LOW)
        parts.append(dot(r.turned_rows[head * HEAD : (head + 1) * HEAD], probs))
    r.context[at] = jnp.transpose(jnp.concatenate(parts, axis=0)).astype(LOW)


def attend_first(r, half):
    per_side = half // QUERIES
    for side in range(2):
        attend(r, side * per_side)
    extras = []
    for block in range(1, per_side):
        for side in range(2):
            step = max(0, block * QUERIES // CHUNK - 2 + side)
            extras.append(at_step(step, lambda block=side * per_side + block: attend(r, block)))
    return extras


def attend_back(r, between=()):
    rows = r.attn_low_in.shape[0]
    heads = r.qkv_w.shape[2] // HEAD
    scale = HEAD ** (-0.5)
    r.grad_context[...] = dot_t(r.attn_low_in[...], r.proj_w[...]).astype(LOW)
    r.turned_rows[...] = turned(r.projected[1])
    clear(r.grad_key, r.grad_value)
    for number in range(rows // QUERIES):
        at = slice(number * QUERIES, (number + 1) * QUERIES)
        queries, context_rows = r.projected[0, at], r.grad_context[at]
        parts = []
        for head in range(heads):
            to = slice(head * QUERIES, (head + 1) * QUERIES)
            r.head_queries[to] = head_lanes(queries, head)
            r.head_context[to] = head_lanes(context_rows, head)
            scores = masked_block(r, r.projected[1], r.head_queries[to], at)
            probability = jnp.exp(scores - r.log_total[head : head + 1, at])
            grad_probs = dot_t(r.projected[2], r.head_context[to])
            inner = jnp.sum(probability * grad_probs, axis=0, keepdims=True)
            grad_scores = (probability * (grad_probs - inner)).astype(LOW)
            r.score_rows[:, to] = grad_scores
            r.prob_rows[:, to] = probability.astype(LOW)
            parts.append(dot(r.turned_rows[head * HEAD : (head + 1) * HEAD], grad_scores))
        r.grad_key[...] += dot(r.score_rows[...], r.head_queries[...])
        r.grad_value[...] += dot(r.prob_rows[...], r.head_context[...])
        r.grad_proj[0, at] = (jnp.transpose(jnp.concatenate(parts, axis=0)) * scale).astype(LOW)
        if number < len(between):
            between[number]()
    r.grad_proj[1] = (r.grad_key[...] * scale).astype(LOW)
    r.grad_proj[2] = r.grad_value[...].astype(LOW)
    for slot, member in ((0, 0), (1, 2)):
        r.qv_sum[slot] = jnp.sum(r.grad_proj[member].astype(F32).reshape(-1, 8, r.qv_sum.shape[2]), axis=0)


def take(ref, blocks):
    return jnp.concatenate([ref[block] for block in blocks], axis=0)


def put(ref, blocks, values):
    count = values.shape[0] // len(blocks)
    for number, block in enumerate(blocks):
        ref[block] = values[number * count : (number + 1) * count]


def proj_stage(r, layer, whole):
    def produce(blocks):
        put(r.proj_line[0], blocks, dot(take(r.context, blocks), r.proj_w[...]).astype(LOW))

    def finish(at, own, total):
        came = r.residual[at if whole else own].astype(F32)
        unit, inverse = normalize(came + total + vector(r.proj_b, layer))
        r.unit_one[own] = unit
        r.inverse_one[own] = inverse
        result = unit * vector(r.first_gain, layer) + vector(r.first_shift, layer)
        r.normed[own] = result
        r.normed_low[at] = result.astype(LOW)

    return stage_of(produce, finish, [r.normed_low], r.proj_line)


def ffn_stage(r, layer, last):
    def produce(blocks):
        pre = dot(take(r.normed_low, blocks), r.up_w[...]) + vector(r.up_b, layer)
        cdf = 0.5 * lax.erf(pre * math.sqrt(0.5)) + 0.5
        act = (pre * cdf).astype(LOW)
        slope = cdf + pre * jnp.exp(-0.5 * pre * pre) * (1.0 / math.sqrt(2 * math.pi))
        put(r.slope, blocks, slope.astype(LOW))
        put(r.act, blocks, act)
        put(r.ffn_line[0], blocks, dot(act, r.down_w[...]).astype(LOW))

    def finish(at, own, total):
        unit, inverse = normalize(r.normed[own] + total + vector(r.down_b, layer))
        gain = vector(r.second_gain, layer)
        result = unit * gain + vector(r.second_shift, layer)
        if last:
            r.mixed_own[own] = result.astype(LOW)
            grad_in = r.cotangent[at].astype(F32)
            grad = norm_back(grad_in, gain, unit, inverse)
            r.grad_second[own] = grad
            r.branch[at] = grad.astype(LOW)
            tally(r.sums.at[0], grad_in * unit)
            tally(r.sums.at[1], grad_in)
            tally(r.sums.at[2], grad.astype(LOW).astype(F32))
        else:
            r.unit_two[own] = unit
            r.inverse_two[own] = inverse
            r.hidden[own] = result
            r.low[at] = result.astype(LOW)

    return stage_of(produce, finish, [r.branch if last else r.low], r.ffn_line)


def ffn_back_stage(r, layer):
    def produce(blocks):
        grad = dot_t(take(r.branch, blocks), r.down_w[...])
        pre = (grad * take(r.slope, blocks).astype(F32)).astype(LOW)
        put(r.pre, blocks, pre)
        tally(r.up_sum, pre.astype(F32))
        put(r.back_line[0], blocks, dot_t(pre, r.up_w[...]).astype(LOW))

    def finish(at, own, total):
        grad_in = r.grad_second[own] + total
        unit = r.unit_one[own]
        grad = norm_back(grad_in, vector(r.first_gain, layer), unit, r.inverse_one[own])
        r.grad_first[own] = grad
        r.attn_low[at] = grad.astype(LOW)
        tally(r.sums.at[3], grad_in * unit)
        tally(r.sums.at[4], grad_in)
        tally(r.sums.at[5], grad.astype(LOW).astype(F32))

    return stage_of(produce, finish, [r.attn_low], r.back_line)


def qkv_back_stage(r, layer, inner):
    def produce(blocks):
        total = sum(dot_t(take(r.grad_proj.at[member], blocks), r.qkv_w[member]) for member in range(3))
        put(r.qkv_line[0], blocks, total.astype(LOW))

    def finish(at, own, total):
        grad_in = r.grad_first_in[own] + total
        if not inner:
            r.grad_low[at] = grad_in.astype(LOW)
            return
        unit = r.unit_two[own]
        grad = norm_back(grad_in, vector(r.second_gain, layer), unit, r.inverse_two[own])
        r.grad_second[own] = grad
        r.branch[at] = grad.astype(LOW)
        tally(r.sums.at[0], grad_in * unit)
        tally(r.sums.at[1], grad_in)
        tally(r.sums.at[2], grad.astype(LOW).astype(F32))

    return stage_of(produce, finish, [r.branch] if inner else [r.grad_low], r.qkv_line)


def columns(piece):
    return pl.ds(pl.multiple_of(piece * PIECE, PIECE), PIECE)


def ffn_grads(r, out, first):
    width, hidden = r.up_w.shape

    def up(piece):
        rows = pl.ds(pl.multiple_of(piece * PIECE, PIECE), PIECE)
        out[rows] = dot_tn(r.normed_low[:, columns(piece)], r.pre[...]).astype(LOW)

    def down(piece):
        rows = pl.ds(pl.multiple_of(width + piece * PIECE, PIECE), PIECE)
        out[rows] = dot_tn(r.act[:, columns(piece)], r.branch[...]).astype(LOW)

    return [(first, width // PIECE, up), (first + width // PIECE, hidden // PIECE, down)]


def attn_grads(r, out, first):
    width, part = r.low_in.shape[1], r.context_in.shape[1]

    def piece_of(piece):
        for member in range(3):
            rows = pl.ds(pl.multiple_of(member * width + piece * part, part), part)
            taken = r.low_in[:, pl.ds(pl.multiple_of(piece * part, part), part)]
            out[rows] = dot_tn(taken, r.grad_proj[member]).astype(LOW)
        rows = pl.ds(pl.multiple_of(3 * width + piece * part, part), part)
        taken = r.attn_low_in[:, pl.ds(pl.multiple_of(piece * part, part), part)]
        out[rows] = dot_tn(r.context_in[...], taken).astype(LOW)

    def all_pieces():
        lax.fori_loop(0, width // part, lambda piece, carry: (piece_of(piece), carry)[1], 0)

    return [at_step(first, all_pieces)]


def at_step(step, work):
    return (step, 1, lambda index: work())


def with_suffix(suffix, named):
    return {name + suffix: value for name, value in named.items()}


def kept_attention(rows, part):
    return dict(
        projected=shape(3, rows, part, kind=LOW),
        log_total=shape(part // HEAD, rows),
        context=shape(rows, part, kind=LOW),
    )


def forward_kernel(size, collective, ins):
    rows, width = ins["low_in_0"].shape
    part, hidden = ins["proj_w_0"].array.shape[1], ins["up_w_0"].array.shape[2]
    half = rows // 2
    chunks = half // CHUNK

    def body(r):
        wait = greet(size)
        clear(r.sums, r.up_sum)
        mark_segments(r)
        below, above = view(r, "_0"), view(r, "_1")
        below.residual = r.low_in_0
        above.low_in, above.residual = r.low_0, r.hidden_0
        r.need("qkv_w_0")
        project(below, 0)
        extras = attend_first(below, half)
        r.need("proj_w_0", "up_w_0", "down_w_0")
        wait()
        line_loop(size, [proj_stage(below, 0, True), ffn_stage(below, 0, False)], extras, 3)
        r.send("projected_0", "context_0", "unit_one_0", "normed_low_0", "act_0", "slope_0", "unit_two_0", "low_0")
        r.need("qkv_w_1")
        project(above, 1)
        extras = attend_first(above, half)
        r.need("proj_w_1", "up_w_1", "down_w_1")
        stages = [proj_stage(above, 1, False), ffn_stage(above, 1, True), ffn_back_stage(above, 1)]
        first = 4 * LAG * (size - 1) + chunks
        line_loop(
            size,
            stages,
            [
                *extras,
                at_step(2 * chunks, lambda: r.send("projected_1", "context_1")),
                *ffn_grads(above, r.ffn_grad, first),
                at_step(first + 2 * width // PIECE, lambda: r.send("ffn_grad", "mixed_own")),
            ],
        )
        r.send("grad_first", "attn_low")

    outs = dict(
        **with_suffix("_0", kept_attention(rows, part)),
        **with_suffix("_1", kept_attention(rows, part)),
        unit_one_0=shape(half, width),
        inverse_one_0=shape(half, 1),
        normed_low_0=shape(rows, width, kind=LOW),
        act_0=shape(rows, hidden, kind=LOW),
        slope_0=shape(rows, hidden, kind=LOW),
        unit_two_0=shape(half, width),
        inverse_two_0=shape(half, 1),
        low_0=shape(rows, width, kind=LOW),
        mixed_own=shape(half, width, kind=LOW),
        grad_first=shape(half, width),
        attn_low=shape(rows, width, kind=LOW),
        ffn_grad=shape(width + hidden, width, kind=LOW),
        up_sum=shape(8, hidden),
        sums=shape(6, 8, width),
    )
    scratch = dict(
        hidden_0=pltpu.VMEM((half, width), F32),
        normed=pltpu.VMEM((half, width), F32),
        turned_rows=pltpu.VMEM((part, rows), LOW),
        seg_cols=pltpu.VMEM((rows, QUERIES), F32),
        unit_one_1=pltpu.VMEM((half, width), F32),
        inverse_one_1=pltpu.VMEM((half, 1), F32),
        normed_low_1=pltpu.VMEM((rows, width), LOW),
        act_1=pltpu.VMEM((rows, hidden), LOW),
        slope_1=pltpu.VMEM((rows, hidden), LOW),
        pre=pltpu.VMEM((rows, hidden), LOW),
        branch=pltpu.VMEM((rows, width), LOW),
        grad_second=pltpu.VMEM((half, width), F32),
        proj_line_0=line_scratch(rows, width),
        ffn_line_0=line_scratch(rows, width),
        proj_line_1=line_scratch(rows, width),
        ffn_line_1=line_scratch(rows, width),
        back_line=line_scratch(rows, width),
    )
    sent = [name for name, out in outs.items() if out.dtype == LOW or name in ("unit_one_0", "unit_two_0", "grad_first")]
    return call(collective, body, ins, outs, scratch, sent=sent)


def backward_kernel(size, chips, collective, layers, ins):
    rows, width = ins["attn_low_1"].array.shape
    part, hidden = ins["proj_w_0"].array.shape[1], ins["up_w"].array.shape[2]
    half = rows // 2
    chunks = half // CHUNK
    span = 2 * LAG * (size - 1)
    ffn_rows, attn_rows = width + hidden, 4 * width
    own_rows = layers * (2 * part + hidden) // width
    count = -(-(own_rows + 6 * layers) // 8) * 8
    teams = 2 * chips

    def row_peer(index):
        row, place = here()
        return (lax.rem(row + index + 1, teams), place)

    def line_peer(index):
        row, place = here()
        return (row, lax.rem(place + index + 1, size))

    def each(number, work):
        def one(index, carry):
            work(index)
            return carry

        lax.fori_loop(0, number, one, 0)

    def body(r):
        row, place = here()
        clear(r.ends, r.sums_0, r.up_sum_0)
        wait = greet(size, line=False, targets=[(teams - 1, row_peer), (size - 1, line_peer)])
        ffn_above = spread_of(chips, r.ffn_whole_1, r.ffn_spread[:5])
        attn_above = spread_of(chips, r.attn_whole_1, r.attn_spread[:5])
        ffn_below = spread_of(chips, r.ffn_whole_0, r.ffn_spread[:2] + r.ffn_spread[5:])
        attn_below = spread_of(chips, r.attn_whole_0, r.attn_spread[:2] + r.attn_spread[5:])
        above, below = view(r, "_1"), view(r, "_0")
        above.grad_first_in, above.attn_low_in = r.grad_first_1, r.attn_low_1
        below.grad_first_in, below.attn_low_in = r.grad_first_0, r.attn_low_0
        middle = types.SimpleNamespace(
            **{**vars(r), "sums": r.sums_0, "up_sum": r.up_sum_0, "grad_first": r.grad_first_0, "attn_low": r.attn_low_0}
        )
        above.sums = r.sums_0
        above.grad_second = middle.grad_second = r.grad_first_0
        below.qkv_line = [*r.qkv_line_1[:2], *r.qkv_sems_0]

        def end_copy(slot, index):
            return pltpu.make_async_remote_copy(
                src_ref=r.small,
                dst_ref=r.ends.at[slot],
                send_sem=r.end_sent.at[slot, index],
                recv_sem=r.end_got.at[slot],
                device_id=line_peer(index),
                device_id_type=MESH,
            )

        def team_copy(index, slot):
            return pltpu.make_async_remote_copy(
                src_ref=r.mine,
                dst_ref=r.others.at[slot],
                send_sem=r.team_sent.at[index],
                recv_sem=r.team_got.at[slot],
                device_id=row_peer(index),
                device_id_type=MESH,
            )

        end_places = ((0, 0), (1, size - 1))
        end = size - 1

        def side_rows(side):
            at, back = (place, place - 1) if side == 0 else (end - place, place + 1)
            return at, back, r.mixed.at[pl.ds(side * half, half)]

        def mixed_copy(side):
            at, back, rows_at = side_rows(side)
            return pltpu.make_async_remote_copy(
                src_ref=rows_at,
                dst_ref=rows_at,
                send_sem=r.mixed_sent.at[side],
                recv_sem=r.mixed_got.at[side],
                device_id=(row, back),
                device_id_type=MESH,
            )

        def mixed_hop(number):
            for side in range(2):
                at, _, rows_at = side_rows(side)

                @pl.when(at == end - number)
                def _():
                    if number:
                        mixed_copy(side).wait_recv()
                    else:
                        rows_at[...] = r.mixed_own[...]
                    mixed_copy(side).start()

        def mixed_settle():
            for side in range(2):
                at, _, _ = side_rows(side)

                @pl.when(at == 0)
                def _():
                    mixed_copy(side).wait_recv()

                @pl.when(at > 0)
                def _():
                    mixed_copy(side).wait_send()

        def small_to_line():
            named = vars(r)
            clear(r.small)
            lines = []
            for layer in range(layers):
                sums = jnp.sum(named["qv_sum_%d" % layer][...], axis=1)
                lines += [sums[0:1], sums[1:2]]
            for layer in range(layers):
                lines += [jnp.sum(named["up_sum_%d" % layer][...], axis=0, keepdims=True)]
            flat = jnp.concatenate(lines, axis=1)
            for number in range(own_rows):
                r.small[number : number + 1] = flat[:, number * width : (number + 1) * width]
            for layer in range(layers):
                sums = jnp.sum(named["sums_%d" % layer][...], axis=1)
                for member in range(6):
                    to = own_rows + member * layers + layer
                    r.small[to : to + 1] = sums[member : member + 1]
            for slot, end in end_places:

                @pl.when(place == end)
                def _():
                    each(size - 1, lambda index: end_copy(slot, index).start())

        def small_to_teams():
            for slot, end in end_places:

                @pl.when(place != end)
                def _():
                    end_copy(slot, 0).wait_recv()

            line_total = r.small[...] + r.ends[0] + r.ends[1]
            number = lax.broadcasted_iota(jnp.int32, (count, width), 0)
            r.mine[...] = jnp.where(number < own_rows, r.small[...], line_total)
            each(teams - 1, lambda index: team_copy(index, row).start())
            r.others[row] = r.mine[...]

        def small_finish():
            each(teams - 1, lambda index: team_copy(index, row_peer(index)[0]).wait_recv())
            r.small_total[...] = lax.fori_loop(
                1, teams, lambda index, total: total + r.others[index], r.others[0]
            )
            each(teams - 1, lambda index: team_copy(index, row).wait_send())
            for slot, end in end_places:

                @pl.when(place == end)
                def _():
                    each(size - 1, lambda index: end_copy(slot, index).wait_send())

        mark_segments(r)
        r.need("proj_w_1", "attn_low_1", "projected_1", "mixed_own", "ffn_grad_1")
        wait()
        ffn_above.to_partner()
        mixed_hop(0)
        attend_back(above, [lambda: None, ffn_above.to_chips])
        r.need("qkv_w_1", "grad_first_1", "unit_two", "context_in_1", "low_in_1")
        r.need("up_w", "down_w", "slope", "unit_one", "act", "normed_low")
        extras = [
            *attn_grads(above, r.attn_whole_1, 2),
            at_step(4, ffn_above.onward),
            at_step(6, attn_above.to_partner),
            at_step(8, ffn_above.give_share),
            at_step(9, attn_above.to_chips),
            at_step(11, ffn_above.pass_on),
            at_step(span - 2, lambda: r.fetch("proj_w_0", "qkv_w_0")),
            at_step(span + 2, attn_above.onward),
            at_step(span + 5, attn_above.give_share),
            at_step(span + 6, ffn_above.to_other_core),
            at_step(span + 8, attn_above.pass_on),
            *ffn_grads(middle, r.ffn_whole_0, span + chunks),
            at_step(span + chunks + 2, lambda: (ffn_above.settle(), r.send("ffn_whole_1"))),
            at_step(2 * span, ffn_below.to_partner),
            at_step(2 * span + 1, attn_above.to_other_core),
            at_step(2 * span + 2, ffn_below.to_chips),
            at_step(2 * span + 5, lambda: (attn_above.settle(), r.send("attn_whole_1"))),
        ]
        stages = [qkv_back_stage(above, 0, True), ffn_back_stage(middle, 0)]
        line_loop(size, stages, extras)
        r.need("proj_w_0", "qkv_w_0", "projected_0")
        mixed_hop(1)
        attend_back(below, [lambda: None, ffn_below.onward])
        ffn_below.give_share()
        r.need("context_in_0", "low_in_0")
        extras = [
            *attn_grads(below, r.attn_whole_0, 0),
            at_step(1, attn_below.to_partner),
            at_step(2, small_to_line),
            *(at_step(3 + 6 * (hop - 2), lambda hop=hop: mixed_hop(hop)) for hop in range(2, end)),
            at_step(3, ffn_below.pass_on),
            at_step(3, attn_below.to_chips),
            at_step(6, small_to_teams),
            at_step(8, attn_below.onward),
            at_step(10, ffn_below.to_other_core),
            at_step(11, attn_below.give_share),
            at_step(13, attn_below.pass_on),
            at_step(14, small_finish),
            at_step(15, lambda: (ffn_below.settle(), r.send("ffn_whole_0"))),
            at_step(17, attn_below.to_other_core),
        ]
        line_loop(size, [qkv_back_stage(below, 0, False)], extras)
        mixed_settle()
        r.send("grad_low", "mixed")
        attn_below.settle()
        r.send("attn_whole_0")

    heads = part // HEAD
    rooms = {"ffn_grad_1": "ffn_whole_1", "qkv_w_0": "qkv_w_1", "proj_w_0": "proj_w_1"}
    outs = dict(
        grad_low=shape(rows, width, kind=LOW),
        mixed=shape(rows, width, kind=LOW),
        ffn_whole_1=shape(ffn_rows, width, kind=LOW),
        attn_whole_1=shape(attn_rows, part, kind=LOW),
        ffn_whole_0=shape(ffn_rows, width, kind=LOW),
        attn_whole_0=shape(attn_rows, part, kind=LOW),
        small_total=shape(count, width),
    )
    scratch = dict(
        seg_cols=pltpu.VMEM((rows, QUERIES), F32),
        turned_rows=pltpu.VMEM((part, rows), LOW),
        grad_context=pltpu.VMEM((rows, part), LOW),
        grad_key=pltpu.VMEM((rows, part), F32),
        grad_value=pltpu.VMEM((rows, part), F32),
        grad_proj=pltpu.VMEM((3, rows, part), LOW),
        head_queries=pltpu.VMEM((heads * QUERIES, part), LOW),
        head_context=pltpu.VMEM((heads * QUERIES, part), LOW),
        score_rows=pltpu.VMEM((rows, heads * QUERIES), LOW),
        prob_rows=pltpu.VMEM((rows, heads * QUERIES), LOW),
        qv_sum_0=pltpu.VMEM((2, 8, part), F32),
        qv_sum_1=pltpu.VMEM((2, 8, part), F32),
        sums_0=pltpu.VMEM((6, 8, width), F32),
        up_sum_0=pltpu.VMEM((8, hidden), F32),
        pre=pltpu.VMEM((rows, hidden), LOW),
        branch=pltpu.VMEM((rows, width), LOW),
        grad_first_0=pltpu.VMEM((half, width), F32),
        attn_low_0=pltpu.VMEM((rows, width), LOW),
        small=pltpu.VMEM((count, width), F32),
        ends=pltpu.VMEM((2, count, width), F32),
        mine=pltpu.VMEM((count, width), F32),
        others=pltpu.VMEM((teams, count, width), F32),
        end_sent=pltpu.SemaphoreType.DMA((2, size - 1)),
        end_got=pltpu.SemaphoreType.DMA((2,)),
        team_sent=pltpu.SemaphoreType.DMA((teams - 1,)),
        team_got=pltpu.SemaphoreType.DMA((teams,)),
        mixed_sent=pltpu.SemaphoreType.DMA((2,)),
        mixed_got=pltpu.SemaphoreType.DMA((2,)),
        qkv_line_1=line_scratch(rows, width),
        back_line=line_scratch(rows, width),
        qkv_sems_0=line_scratch(rows, width)[2:],
        ffn_spread=Spread.scratch(chips, ffn_rows, width),
        attn_spread=Spread.scratch(chips, attn_rows, part),
    )
    return call(collective, body, ins, outs, scratch, rooms, ("qkv_w_0", "proj_w_0"), [*outs][:-1]), own_rows


def assemble(attn_wholes, ffn_wholes, mixed, grad_low, small, own_rows, part):
    layers = len(attn_wholes)
    rows, width = mixed.shape
    hidden = ffn_wholes[0].shape[0] - width
    steps = 4
    cut = width // steps

    def for_layer(number, spec_of):
        def index(layer, step):
            return spec_of(jnp.where(layer == number, step, jnp.where(layer < number, 0, steps - 1)))

        return index

    ins, in_specs = [], []
    for number in range(layers):
        ins += [
            attn_wholes[number].reshape(4, width, part),
            attn_wholes[number].reshape(-1, part, part),
            ffn_wholes[number].reshape(-1, width, width),
        ]
        in_specs += [
            pl.BlockSpec((3, cut, part), for_layer(number, lambda step: (0, step, 0))),
            pl.BlockSpec((width // part, part // steps, part), for_layer(number, lambda step: (3, step, 0))),
            pl.BlockSpec((1 + hidden // width, cut, width), for_layer(number, lambda step: (0, step, 0))),
        ]
    slab = rows // (layers * steps)
    ins += [mixed, grad_low, small]
    row_spec = pl.BlockSpec((slab, width), lambda layer, step: (layer * steps + step, 0))
    in_specs += [row_spec, row_spec, pl.BlockSpec(small.shape, lambda layer, step: (0, 0))]
    def all_of(*dims):
        return pl.BlockSpec(dims, lambda layer, step: (0,) * len(dims))

    out_shape = [
        shape(rows, width),
        shape(rows, width),
        shape(layers, 3, width, part),
        shape(layers, part, width),
        shape(layers, width, hidden),
        shape(layers, hidden, width),
        shape(layers, 2, part),
        shape(layers, hidden),
    ] + [shape(layers, width)] * 6
    out_specs = [
        row_spec,
        row_spec,
        pl.BlockSpec((1, 3, cut, part), lambda layer, step: (layer, 0, step, 0)),
        pl.BlockSpec((1, part // steps, width), lambda layer, step: (layer, step, 0)),
        pl.BlockSpec((1, cut, hidden), lambda layer, step: (layer, step, 0)),
        pl.BlockSpec((1, cut, width), lambda layer, step: (layer, step, 0)),
        all_of(layers, 2, part),
        all_of(layers, hidden),
    ] + [all_of(layers, width)] * 6

    def body(*refs):
        sources = refs[: 3 * layers]
        mixed_in, grad_in, small_in = refs[3 * layers : 3 * layers + 3]
        mixed_out, grad_out, qkv, proj, up, down, qv, up_b, *norms = refs[3 * layers + 3 :]
        mixed_out[...] = mixed_in[...].astype(F32)
        grad_out[...] = grad_in[...].astype(F32)
        for number in range(layers):
            attn_in, proj_in, ffn_in = sources[3 * number : 3 * number + 3]

            @pl.when(pl.program_id(0) == number)
            def _():
                qkv[0] = attn_in[...].astype(F32)
                for block in range(width // part):
                    proj[0, :, block * part : (block + 1) * part] = proj_in[block].astype(F32)
                up[0] = ffn_in[0].astype(F32)
                down[0] = ffn_in[1].astype(F32)

        @pl.when((pl.program_id(0) == 0) & (pl.program_id(1) == 0))
        def _():
            values = small_in[...]
            flat = jnp.concatenate([values[n : n + 1] for n in range(own_rows)], axis=1)
            for layer in range(layers):
                for member in range(2):
                    at = (2 * layer + member) * part
                    qv[layer, member : member + 1] = flat[:, at : at + part]
                at = 2 * layers * part + layer * hidden
                up_b[layer : layer + 1] = flat[:, at : at + hidden]
            for member, norm in enumerate(norms):
                norm[...] = values[own_rows + member * layers : own_rows + (member + 1) * layers]

    return pl.pallas_call(
        body,
        grid=(layers, steps),
        out_shape=out_shape,
        in_specs=in_specs,
        out_specs=out_specs,
        compiler_params=pltpu.CompilerParams(vmem_limit_bytes=60 << 20),
    )(*ins)


def local(
    tokens,
    segment_ids,
    cotangent,
    qkv_weight,
    qv_bias,
    proj_weight,
    proj_bias,
    first_gain,
    first_shift,
    up_weight,
    up_bias,
    down_weight,
    down_bias,
    second_gain,
    second_shift,
):
    seq_count, length, width = tokens.shape
    rows = seq_count * length
    layers = qkv_weight.shape[0]
    size = lax.axis_size("tensor")
    chips = lax.axis_size("dp") // 2
    part = qkv_weight.shape[-1]
    qkv_stack = jnp.transpose(qkv_weight, (0, 2, 1, 3))
    low = tokens.reshape(rows, width)
    weights = dict(qkv_w=qkv_stack, proj_w=proj_weight, up_w=up_weight, down_w=down_weight)
    ins = dict(
        low_in_0=low,
        cotangent=cotangent.reshape(rows, width),
        seg_row=segment_ids,
        qv_bias=qv_bias,
        proj_b=proj_bias,
        first_gain=first_gain,
        first_shift=first_shift,
        up_b=up_bias,
        down_b=down_bias,
        second_gain=second_gain,
        second_shift=second_shift,
    )
    for layer in range(layers):
        for name, array in weights.items():
            ins["%s_%d" % (name, layer)] = Layer(array, layer)
    done = forward_kernel(size, 0, ins)
    last, own_rows = backward_kernel(
        size,
        chips,
        1,
        layers,
        dict(
            seg_row=segment_ids,
            log_total_0=done.log_total_0,
            log_total_1=done.log_total_1,
            sums_1=done.sums,
            up_sum_1=done.up_sum,
            inverse_two=done.inverse_two_0,
            inverse_one=done.inverse_one_0,
            first_gain=first_gain,
            second_gain=second_gain,
            proj_w_1=Layer(proj_weight, 1),
            attn_low_1=whole(done.attn_low),
            projected_1=whole(done.projected_1),
            mixed_own=whole(done.mixed_own),
            ffn_grad_1=whole(done.ffn_grad),
            qkv_w_1=Layer(qkv_stack, 1),
            grad_first_1=whole(done.grad_first),
            unit_two=whole(done.unit_two_0),
            context_in_1=whole(done.context_1),
            low_in_1=whole(done.low_0),
            up_w=Layer(up_weight, 0),
            down_w=Layer(down_weight, 0),
            slope=whole(done.slope_0),
            unit_one=whole(done.unit_one_0),
            act=whole(done.act_0),
            normed_low=whole(done.normed_low_0),
            proj_w_0=Layer(proj_weight, 0),
            qkv_w_0=Layer(qkv_stack, 0),
            projected_0=whole(done.projected_0),
            context_in_0=whole(done.context_0),
            low_in_0=whole(low),
        ),
    )
    ffn_wholes = [last.ffn_whole_0, last.ffn_whole_1]
    attn_wholes = [last.attn_whole_0, last.attn_whole_1]

    mixed, input_grad, qkv, proj, up, down, qv, up_b, *norms = assemble(
        attn_wholes, ffn_wholes, last.mixed, last.grad_low, last.small_total, own_rows, part
    )
    return (
        mixed.reshape(tokens.shape),
        input_grad.reshape(tokens.shape),
        jnp.transpose(qkv, (0, 2, 1, 3)),
        qv,
        proj,
        norms[5],
        norms[3],
        norms[4],
        up,
        up_b,
        down,
        norms[2],
        norms[0],
        norms[1],
    )


def solution(mesh):
    return jax.shard_map(
        local,
        mesh=mesh,
        in_specs=(
            P("dp", None, None),
            P("dp", None),
            P("dp", None, None),
            P(None, None, None, "tensor"),
            P(None, None, "tensor"),
            P(None, "tensor", None),
            P(),
            P(),
            P(),
            P(None, None, "tensor"),
            P(None, "tensor"),
            P(None, "tensor", None),
            P(),
            P(),
            P(),
        ),
        out_specs=(
            P("dp", None, None),
            P("dp", None, None),
            P(None, None, None, "tensor"),
            P(None, None, "tensor"),
            P(None, "tensor", None),
            P(),
            P(),
            P(),
            P(None, None, "tensor"),
            P(None, "tensor"),
            P(None, "tensor", None),
            P(),
            P(),
            P(),
        ),
        check_vma=False,
    )
```

profile of v0, /device:TPU:0, one launch (start us, length us, event | category | flops | bytes accessed | tf_op | source)
XLA Modules:
  0.0 333.4 jit_solution(8562886158407198304)
XLA Ops:
  0.6 164.8 %shard_map.254 = (bf16[3,512,256]{2,1,0:T(8,128)(2,1)}, f32[4,512]{1,0:T(4,128)}, bf16[512,256]{1,0:T(8,128)(2,1)}, bf16[3,512,256]{2,1,0:T(8,128)(2,1)}, f32[4,...) custom-call(bf16[512,1024]{1,0:T(8,128)(2,1)} %bitcast.22, ...), custom_call_target="tpu_custom_call" | custom-call | tf_op jit(solution)/shard_map/pallas_call | solution.py:518
  165.5 151.4 %shard_map.255 = (bf16[512,1024]{1,0:T(8,128)(2,1)}, bf16[512,1024]{1,0:T(8,128)(2,1)}, bf16[2048,1024]{1,0:T(8,128)(2,1)}, bf16[4096,256]{1,0:T(8,128)(2,1)}, b...) custom-call(s32[1,512]{1,0:T(1,128)} %refs_0_.1, f32[4,512]{1,0:T(4,128)} %get-tuple-element.55.refs_1_, ...), custom_call_target="tpu_custom_call" | custom-call | tf_op jit(solution)/shard_map/pallas_call | solution.py:518
  316.9 16.3 %shard_map.256 = (f32[512,1024]{1,0:T(8,128)}, f32[512,1024]{1,0:T(8,128)}, f32[2,3,1024,256]{3,2,1,0:T(8,128)}, f32[2,256,1024]{2,1,0:T(8,128)}, f32[2,1024,102...) custom-call(bf16[4,1024,256]{2,1,0:T(8,128)(2,1)} %bitcast.18, ...), custom_call_target="tpu_custom_call" | custom-call | tf_op jit(solution)/shard_map/pallas_call | solution.py:1234
where the time goes:
time: 334 us; the launch traced here: 333 us
  Pallas kernels  333 us (100%)
    pallas_call x2, Pallas kernels, call(): pl.pallas_call(run, out_shape=list(outs.values()), in_specs=[pl.BlockSpec...  316 us
    pallas_call x1, Pallas kernels, assemble(): pl.pallas_call(body, grid=(layers, steps), out_shape=out_shape, in_specs=...  16.3 us

commit v1 on v0

--- a/solution.py
+++ b/solution.py
@@ -81,6 +81,11 @@
 def partner():
     row, place = here()
     return (row + 1 - 2 * lax.rem(row, 2), place)
+
+
+def plane_peer(chips, index):
+    row, place = here()
+    return (lax.rem(row // 2 + index + 1, chips) * 2 + lax.rem(row, 2), place)
 
 
 def line_loop(size, stages, extras=(), lag=LAG):
@@ -150,8 +155,7 @@
                     @pl.when(at > 0)
                     def _():
                         rows = rows_of(side, chunk)
-                        total = stage.part[rows].astype(F32) + stage.recv[rows].astype(F32)
-                        stage.part[rows] = total.astype(LOW)
+                        stage.part[rows] = stage.part[rows] + stage.recv[rows]
 
                     sum_copy(stage, side, chunk, onward).start()
 
@@ -278,10 +282,33 @@
 
         by_rows(self.half, add)
 
+    def settle_sum(self):
+        self.settle_there()
+        pl.semaphore_wait(self.free, 1)
+
+    def give_share(self):
+        self.sum_share(self.grads, self.own_rows())
+        self.start_back()
+
+    def keep_share(self, share):
+        count = share.shape[0] // len(self.own_rows())
+        for number, base in enumerate(self.own_rows()):
+
+            def keep(rows, first, number=number, base=base):
+                came = share[self.rows(number * count + first, rows.size)]
+                self.grads[self.rows(base + first, rows.size)] = came
+
+            by_rows(count, keep)
+        self.summed = False
+        self.start_back()
+
+    summed = True
+
     def to_other_core(self):
         self.take_back()
-        self.settle_chips()
-        pl.semaphore_wait(self.free, 1)
+        if self.summed:
+            self.settle_sum()
+        self.settle_back()
         self.last_copy().start()
 
     def settle(self):
@@ -318,7 +345,10 @@
     def onward(self):
         pass
 
-    def give_share(self):
+    def own_rows(self):
+        return [self.core * self.half + self.chip * (self.half // self.chips)]
+
+    def sum_share(self, target, starts):
         self.each(lambda index: self.far_copy(index).wait_recv())
         count = self.half // self.chips
         base = self.chip * count
@@ -329,9 +359,11 @@
 
             own = self.near[self.rows(base + first, rows.size)].astype(F32)
             total = lax.fori_loop(0, self.chips - 1, one, own)
-            self.grads[self.rows(self.core * self.half + base + first, rows.size)] = total.astype(LOW)
+            target[self.rows(starts[0] + first, rows.size)] = total.astype(LOW)
 
         by_rows(count, add)
+
+    def start_back(self):
         self.each(lambda index: self.back_copy(index).start())
 
     def pass_on(self):
@@ -340,8 +372,10 @@
     def take_back(self):
         self.each(lambda index: self.back_copy(index).wait_recv())
 
-    def settle_chips(self):
+    def settle_there(self):
         self.each(lambda index: self.far_copy(index).wait_send())
+
+    def settle_back(self):
         self.each(lambda index: self.back_copy(index).wait_send())
 
 
@@ -398,18 +432,23 @@
             by_rows(self.quarter, add)
             self.second_copy(side).start()
 
-    def give_share(self):
+    def own_rows(self):
+        return [self.core * self.half + self.own[side] for side in range(2)]
+
+    def sum_share(self, target, starts):
         for side in range(2):
             self.second_copy(side).wait_recv()
-            base = self.own[side]
-
-            def add(rows, first, side=side, base=base):
+            base, start = self.own[side], starts[side]
+
+            def add(rows, first, side=side, base=base, start=start):
                 came = self.far[self.rows(2 * self.quarter + side * self.eighth + first, rows.size)]
-                total = self.near[self.rows(base + first, rows.size)].astype(F32) + came.astype(F32)
-                to = self.rows(self.core * self.half + base + first, rows.size)
-                self.grads[to] = total.astype(LOW)
+                own = self.near[self.rows(base + first, rows.size)]
+                target[self.rows(start + first, rows.size)] = own + came
 
             by_rows(self.eighth, add)
+
+    def start_back(self):
+        for side in range(2):
             self.share_copy(side).start()
 
     def pass_on(self):
@@ -421,10 +460,13 @@
         for side in range(2):
             self.pass_copy(side).wait_recv()
 
-    def settle_chips(self):
+    def settle_there(self):
         for side in range(2):
             self.first_copy(side).wait_send()
             self.second_copy(side).wait_send()
+
+    def settle_back(self):
+        for side in range(2):
             self.share_copy(side).wait_send()
             self.pass_copy(side).wait_send()
 
@@ -773,7 +815,13 @@
         rows = pl.ds(pl.multiple_of(width + piece * PIECE, PIECE), PIECE)
         out[rows] = dot_tn(r.act[:, columns(piece)], r.branch[...]).astype(LOW)
 
-    return [(first, width // PIECE, up), (first + width // PIECE, hidden // PIECE, down)]
+    def all_of(pieces, work):
+        lax.fori_loop(0, pieces, lambda piece, carry: (work(piece), carry)[1], 0)
+
+    return [
+        at_step(first, lambda: all_of(width // PIECE, up)),
+        at_step(first + 1, lambda: all_of(hidden // PIECE, down)),
+    ]
 
 
 def attn_grads(r, out, first):
@@ -810,14 +858,15 @@
     )
 
 
-def forward_kernel(size, collective, ins):
+def forward_kernel(size, chips, collective, ins):
     rows, width = ins["low_in_0"].shape
     part, hidden = ins["proj_w_0"].array.shape[1], ins["up_w_0"].array.shape[2]
     half = rows // 2
     chunks = half // CHUNK
 
     def body(r):
-        wait = greet(size)
+        wait = greet(size, targets=[(1, lambda index: partner()), (chips - 1, lambda index: plane_peer(chips, index))])
+        ffn_sum = spread_of(chips, r.ffn_grad, r.ffn_spread[:5])
         clear(r.sums, r.up_sum)
         mark_segments(r)
         below, above = view(r, "_0"), view(r, "_1")
@@ -835,7 +884,7 @@
         extras = attend_first(above, half)
         r.need("proj_w_1", "up_w_1", "down_w_1")
         stages = [proj_stage(above, 1, False), ffn_stage(above, 1, True), ffn_back_stage(above, 1)]
-        first = 4 * LAG * (size - 1) + chunks
+        first = 4 * 3 * (size - 1) + chunks
         line_loop(
             size,
             stages,
@@ -843,10 +892,16 @@
                 *extras,
                 at_step(2 * chunks, lambda: r.send("projected_1", "context_1")),
                 *ffn_grads(above, r.ffn_grad, first),
-                at_step(first + 2 * width // PIECE, lambda: r.send("ffn_grad", "mixed_own")),
+                at_step(first + 2, lambda: (ffn_sum.to_partner(), r.send("mixed_own"))),
+                at_step(first + 5, ffn_sum.to_chips),
+                at_step(first + 15, ffn_sum.onward),
             ],
+            3,
         )
         r.send("grad_first", "attn_low")
+        share = r.ffn_share.shape[0]
+        ffn_sum.sum_share(r.ffn_share, [0, share // 2])
+        ffn_sum.settle_sum()
 
     outs = dict(
         **with_suffix("_0", kept_attention(rows, part)),
@@ -862,7 +917,7 @@
         mixed_own=shape(half, width, kind=LOW),
         grad_first=shape(half, width),
         attn_low=shape(rows, width, kind=LOW),
-        ffn_grad=shape(width + hidden, width, kind=LOW),
+        ffn_share=shape((width + hidden) // 2 // chips, width, kind=LOW),
         up_sum=shape(8, hidden),
         sums=shape(6, 8, width),
     )
@@ -884,8 +939,10 @@
         proj_line_1=line_scratch(rows, width),
         ffn_line_1=line_scratch(rows, width),
         back_line=line_scratch(rows, width),
+        ffn_grad=pltpu.VMEM((width + hidden, width), LOW),
+        ffn_spread=Spread.scratch(chips, width + hidden, width),
     )
-    sent = [name for name, out in outs.items() if out.dtype == LOW or name in ("unit_one_0", "unit_two_0", "grad_first")]
+    sent = [name for name, out in outs.items() if out.dtype == LOW and name != "ffn_share" or name in ("unit_one_0", "unit_two_0", "grad_first")]
     return call(collective, body, ins, outs, scratch, sent=sent)
 
 
@@ -1044,54 +1101,53 @@
                     each(size - 1, lambda index: end_copy(slot, index).wait_send())
 
         mark_segments(r)
-        r.need("proj_w_1", "attn_low_1", "projected_1", "mixed_own", "ffn_grad_1")
+        r.need("proj_w_1", "attn_low_1", "projected_1", "mixed_own")
         wait()
-        ffn_above.to_partner()
+        ffn_above.keep_share(r.ffn_share_1)
         mixed_hop(0)
-        attend_back(above, [lambda: None, ffn_above.to_chips])
+        attend_back(above)
         r.need("qkv_w_1", "grad_first_1", "unit_two", "context_in_1", "low_in_1")
         r.need("up_w", "down_w", "slope", "unit_one", "act", "normed_low")
         extras = [
             *attn_grads(above, r.attn_whole_1, 2),
-            at_step(4, ffn_above.onward),
-            at_step(6, attn_above.to_partner),
-            at_step(8, ffn_above.give_share),
-            at_step(9, attn_above.to_chips),
-            at_step(11, ffn_above.pass_on),
-            at_step(span - 2, lambda: r.fetch("proj_w_0", "qkv_w_0")),
-            at_step(span + 2, attn_above.onward),
-            at_step(span + 5, attn_above.give_share),
-            at_step(span + 6, ffn_above.to_other_core),
-            at_step(span + 8, attn_above.pass_on),
-            *ffn_grads(middle, r.ffn_whole_0, span + chunks),
-            at_step(span + chunks + 2, lambda: (ffn_above.settle(), r.send("ffn_whole_1"))),
-            at_step(2 * span, ffn_below.to_partner),
-            at_step(2 * span + 1, attn_above.to_other_core),
-            at_step(2 * span + 2, ffn_below.to_chips),
-            at_step(2 * span + 5, lambda: (attn_above.settle(), r.send("attn_whole_1"))),
+            at_step(span, lambda: r.fetch("proj_w_0", "qkv_w_0")),
+            *ffn_grads(middle, r.ffn_whole_0, 6 * (size - 1) + chunks),
+            at_step(3, ffn_above.pass_on),
+            at_step(5, attn_above.to_partner),
+            at_step(8, attn_above.to_chips),
+            at_step(12, ffn_above.to_other_core),
+            at_step(15, attn_above.onward),
+            at_step(16, lambda: (ffn_above.settle(), r.send("ffn_whole_1"))),
+            at_step(6 * (size - 1) + 1, attn_above.give_share),
+            at_step(6 * (size - 1) + 5, attn_above.pass_on),
+            at_step(6 * (size - 1) + 10, attn_above.to_other_core),
+            at_step(6 * (size - 1) + 11, ffn_below.to_partner),
+            at_step(6 * (size - 1) + 13, lambda: (attn_above.settle(), r.send("attn_whole_1"))),
+            at_step(6 * (size - 1) + 14, ffn_below.to_chips),
+            at_step(12 * (size - 1) + 6, ffn_below.onward),
         ]
         stages = [qkv_back_stage(above, 0, True), ffn_back_stage(middle, 0)]
-        line_loop(size, stages, extras)
+        line_loop(size, stages, extras, 3)
         r.need("proj_w_0", "qkv_w_0", "projected_0")
         mixed_hop(1)
-        attend_back(below, [lambda: None, ffn_below.onward])
+        attend_back(below)
         ffn_below.give_share()
         r.need("context_in_0", "low_in_0")
         extras = [
             *attn_grads(below, r.attn_whole_0, 0),
+            at_step(2, small_to_line),
+            *(at_step(4 + 6 * (hop - 2), lambda hop=hop: mixed_hop(hop)) for hop in range(2, end)),
+            at_step(7, small_to_teams),
+            at_step(15, small_finish),
             at_step(1, attn_below.to_partner),
-            at_step(2, small_to_line),
-            *(at_step(3 + 6 * (hop - 2), lambda hop=hop: mixed_hop(hop)) for hop in range(2, end)),
             at_step(3, ffn_below.pass_on),
             at_step(3, attn_below.to_chips),
-            at_step(6, small_to_teams),
-            at_step(8, attn_below.onward),
-            at_step(10, ffn_below.to_other_core),
-            at_step(11, attn_below.give_share),
-            at_step(13, attn_below.pass_on),
-            at_step(14, small_finish),
-            at_step(15, lambda: (ffn_below.settle(), r.send("ffn_whole_0"))),
-            at_step(17, attn_below.to_other_core),
+            at_step(9, ffn_below.to_other_core),
+            at_step(9, attn_below.onward),
+            at_step(11, lambda: (ffn_below.settle(), r.send("ffn_whole_0"))),
+            at_step(12, attn_below.give_share),
+            at_step(14, attn_below.pass_on),
+            at_step(18, attn_below.to_other_core),
         ]
         line_loop(size, [qkv_back_stage(below, 0, False)], extras)
         mixed_settle()
@@ -1100,7 +1156,7 @@
         r.send("attn_whole_0")
 
     heads = part // HEAD
-    rooms = {"ffn_grad_1": "ffn_whole_1", "qkv_w_0": "qkv_w_1", "proj_w_0": "proj_w_1"}
+    rooms = {"qkv_w_0": "qkv_w_1", "proj_w_0": "proj_w_1"}
     outs = dict(
         grad_low=shape(rows, width, kind=LOW),
         mixed=shape(rows, width, kind=LOW),
@@ -1283,7 +1339,7 @@
     for layer in range(layers):
         for name, array in weights.items():
             ins["%s_%d" % (name, layer)] = Layer(array, layer)
-    done = forward_kernel(size, 0, ins)
+    done = forward_kernel(size, chips, 0, ins)
     last, own_rows = backward_kernel(
         size,
         chips,
@@ -1294,6 +1350,7 @@
             log_total_0=done.log_total_0,
             log_total_1=done.log_total_1,
             sums_1=done.sums,
+            ffn_share_1=done.ffn_share,
             up_sum_1=done.up_sum,
             inverse_two=done.inverse_two_0,
             inverse_one=done.inverse_one_0,
@@ -1303,7 +1360,6 @@
             attn_low_1=whole(done.attn_low),
             projected_1=whole(done.projected_1),
             mixed_own=whole(done.mixed_own),
-            ffn_grad_1=whole(done.ffn_grad),
             qkv_w_1=Layer(qkv_stack, 1),
             grad_first_1=whole(done.grad_first),
             unit_two=whole(done.unit_two_0),

time: 334 us -> 322 us (0.964)
  Pallas kernels: 333 us -> 321 us
    pallas_call x2, Pallas kernels: 316 us -> 305 us  [call(): pl.pallas_call(run, out_shape=list(outs.values()), in_specs=[pl.BlockSpec...]
where the time goes in v1:
time: 322 us
  Pallas kernels  321 us (100%)
    pallas_call x2, Pallas kernels, call(): pl.pallas_call(run, out_shape=list(outs.values()), in_specs=[pl.BlockSpec...  305 us
    pallas_call x1, Pallas kernels, assemble(): pl.pallas_call(body, grid=(layers, steps), out_shape=out_shape, in_specs=...  16.3 us

profile of v1, /device:TPU:0, one launch (start us, length us, event | category | flops | bytes accessed | tf_op | source)
XLA Modules:
  0.0 321.9 jit_solution(3970608809136028523)
XLA Ops:
  0.6 168.1 %shard_map.254 = (bf16[3,512,256]{2,1,0:T(8,128)(2,1)}, f32[4,512]{1,0:T(4,128)}, bf16[512,256]{1,0:T(8,128)(2,1)}, bf16[3,512,256]{2,1,0:T(8,128)(2,1)}, f32[4,...) custom-call(bf16[512,1024]{1,0:T(8,128)(2,1)} %bitcast.22, ...), custom_call_target="tpu_custom_call" | custom-call | tf_op jit(solution)/shard_map/pallas_call | solution.py:560
  168.8 136.6 %shard_map.255 = (bf16[512,1024]{1,0:T(8,128)(2,1)}, bf16[512,1024]{1,0:T(8,128)(2,1)}, bf16[2048,1024]{1,0:T(8,128)(2,1)}, bf16[4096,256]{1,0:T(8,128)(2,1)}, b...) custom-call(s32[1,512]{1,0:T(1,128)} %refs_0_.1, f32[4,512]{1,0:T(4,128)} %get-tuple-element.55.refs_1_, ...), custom_call_target="tpu_custom_call" | custom-call | tf_op jit(solution)/shard_map/pallas_call | solution.py:560
  305.4 16.3 %shard_map.256 = (f32[512,1024]{1,0:T(8,128)}, f32[512,1024]{1,0:T(8,128)}, f32[2,3,1024,256]{3,2,1,0:T(8,128)}, f32[2,256,1024]{2,1,0:T(8,128)}, f32[2,1024,102...) custom-call(bf16[4,1024,256]{2,1,0:T(8,128)(2,1)} %bitcast.18, ...), custom_call_target="tpu_custom_call" | custom-call | tf_op jit(solution)/shard_map/pallas_call | solution.py:1290

commit v2 on v1

--- a/solution.py
+++ b/solution.py
@@ -163,9 +163,10 @@
                 def _():
                     rows = rows_of(side, chunk)
                     own = pl.ds(pl.multiple_of(chunk * CHUNK, CHUNK), CHUNK)
-                    stage.finish(rows, own, stage.part[rows].astype(F32) + stage.recv[rows].astype(F32))
+                    rest = stage.finish(rows, own, stage.part[rows].astype(F32) + stage.recv[rows].astype(F32))
                     for which in range(len(stage.outs)):
                         row_copy(stage, which, side, chunk, back).start()
+                    rest()
 
     def step(now, carry):
         for number, stage in enumerate(stages):
@@ -205,6 +206,10 @@
         return carry
 
     lax.fori_loop(0, chunks, drain, 0)
+
+
+def chunk_rows(half, chunk):
+    return [pl.ds(pl.multiple_of(side * half + chunk * CHUNK, CHUNK), CHUNK) for side in range(2)]
 
 
 def by_rows(count, work, block=32):
@@ -628,14 +633,14 @@
     return jnp.where(same, dot_t(keys, queries) * HEAD ** (-0.5), masked_value)
 
 
-def project(r, layer):
+def project(r, layer, blocks):
     bias = r.qv_bias[layer].astype(F32)
+    taken = take(r.low_in, blocks)
     for member in range(3):
-        rows = dot(r.low_in[...], r.qkv_w[member])
+        rows = dot(taken, r.qkv_w[member])
         if member != 1:
             rows += bias[member // 2 : member // 2 + 1]
-        r.projected[member] = rows.astype(LOW)
-    r.turned_rows[...] = turned(r.projected[2])
+        put(r.projected.at[member], blocks, rows.astype(LOW))
 
 
 def attend(r, block):
@@ -656,6 +661,7 @@
 
 def attend_first(r, half):
     per_side = half // QUERIES
+    r.turned_rows[...] = turned(r.projected[2])
     for side in range(2):
         attend(r, side * per_side)
     extras = []
@@ -666,11 +672,14 @@
     return extras
 
 
+def context_back(r, blocks):
+    put(r.grad_context, blocks, dot_t(take(r.attn_low_in, blocks), r.proj_w[...]).astype(LOW))
+
+
 def attend_back(r, between=()):
     rows = r.attn_low_in.shape[0]
     heads = r.qkv_w.shape[2] // HEAD
     scale = HEAD ** (-0.5)
-    r.grad_context[...] = dot_t(r.attn_low_in[...], r.proj_w[...]).astype(LOW)
     r.turned_rows[...] = turned(r.projected[1])
     clear(r.grad_key, r.grad_value)
     for number in range(rows // QUERIES):
@@ -717,11 +726,15 @@
     def finish(at, own, total):
         came = r.residual[at if whole else own].astype(F32)
         unit, inverse = normalize(came + total + vector(r.proj_b, layer))
-        r.unit_one[own] = unit
-        r.inverse_one[own] = inverse
         result = unit * vector(r.first_gain, layer) + vector(r.first_shift, layer)
-        r.normed[own] = result
         r.normed_low[at] = result.astype(LOW)
+
+        def rest():
+            r.unit_one[own] = unit
+            r.inverse_one[own] = inverse
+            r.normed[own] = result
+
+        return rest
 
     return stage_of(produce, finish, [r.normed_low], r.proj_line)
 
@@ -741,19 +754,25 @@
         gain = vector(r.second_gain, layer)
         result = unit * gain + vector(r.second_shift, layer)
         if last:
-            r.mixed_own[own] = result.astype(LOW)
             grad_in = r.cotangent[at].astype(F32)
             grad = norm_back(grad_in, gain, unit, inverse)
-            r.grad_second[own] = grad
             r.branch[at] = grad.astype(LOW)
-            tally(r.sums.at[0], grad_in * unit)
-            tally(r.sums.at[1], grad_in)
-            tally(r.sums.at[2], grad.astype(LOW).astype(F32))
         else:
-            r.unit_two[own] = unit
-            r.inverse_two[own] = inverse
-            r.hidden[own] = result
             r.low[at] = result.astype(LOW)
+
+        def rest():
+            if last:
+                r.mixed_own[own] = result.astype(LOW)
+                r.grad_second[own] = grad
+                tally(r.sums.at[0], grad_in * unit)
+                tally(r.sums.at[1], grad_in)
+                tally(r.sums.at[2], grad.astype(LOW).astype(F32))
+            else:
+                r.unit_two[own] = unit
+                r.inverse_two[own] = inverse
+                r.hidden[own] = result
+
+        return rest
 
     return stage_of(produce, finish, [r.branch if last else r.low], r.ffn_line)
 
@@ -770,11 +789,15 @@
         grad_in = r.grad_second[own] + total
         unit = r.unit_one[own]
         grad = norm_back(grad_in, vector(r.first_gain, layer), unit, r.inverse_one[own])
-        r.grad_first[own] = grad
         r.attn_low[at] = grad.astype(LOW)
-        tally(r.sums.at[3], grad_in * unit)
-        tally(r.sums.at[4], grad_in)
-        tally(r.sums.at[5], grad.astype(LOW).astype(F32))
+
+        def rest():
+            r.grad_first[own] = grad
+            tally(r.sums.at[3], grad_in * unit)
+            tally(r.sums.at[4], grad_in)
+            tally(r.sums.at[5], grad.astype(LOW).astype(F32))
+
+        return rest
 
     return stage_of(produce, finish, [r.attn_low], r.back_line)
 
@@ -788,14 +811,18 @@
         grad_in = r.grad_first_in[own] + total
         if not inner:
             r.grad_low[at] = grad_in.astype(LOW)
-            return
+            return lambda: None
         unit = r.unit_two[own]
         grad = norm_back(grad_in, vector(r.second_gain, layer), unit, r.inverse_two[own])
-        r.grad_second[own] = grad
         r.branch[at] = grad.astype(LOW)
-        tally(r.sums.at[0], grad_in * unit)
-        tally(r.sums.at[1], grad_in)
-        tally(r.sums.at[2], grad.astype(LOW).astype(F32))
+
+        def rest():
+            r.grad_second[own] = grad
+            tally(r.sums.at[0], grad_in * unit)
+            tally(r.sums.at[1], grad_in)
+            tally(r.sums.at[2], grad.astype(LOW).astype(F32))
+
+        return rest
 
     return stage_of(produce, finish, [r.branch] if inner else [r.grad_low], r.qkv_line)
 
@@ -873,14 +900,17 @@
         below.residual = r.low_in_0
         above.low_in, above.residual = r.low_0, r.hidden_0
         r.need("qkv_w_0")
-        project(below, 0)
+        project(below, 0, [slice(0, rows)])
         extras = attend_first(below, half)
-        r.need("proj_w_0", "up_w_0", "down_w_0")
+        r.need("proj_w_0", "up_w_0", "down_w_0", "qkv_w_1")
         wait()
+
+        def project_chunk(chunk):
+            project(above, 1, chunk_rows(half, chunk))
+
+        extras.append((4 * 3 * (size - 1), chunks, project_chunk))
         line_loop(size, [proj_stage(below, 0, True), ffn_stage(below, 0, False)], extras, 3)
         r.send("projected_0", "context_0", "unit_one_0", "normed_low_0", "act_0", "slope_0", "unit_two_0", "low_0")
-        r.need("qkv_w_1")
-        project(above, 1)
         extras = attend_first(above, half)
         r.need("proj_w_1", "up_w_1", "down_w_1")
         stages = [proj_stage(above, 1, False), ffn_stage(above, 1, True), ffn_back_stage(above, 1)]
@@ -1105,6 +1135,7 @@
         wait()
         ffn_above.keep_share(r.ffn_share_1)
         mixed_hop(0)
+        context_back(above, [slice(0, rows)])
         attend_back(above)
         r.need("qkv_w_1", "grad_first_1", "unit_two", "context_in_1", "low_in_1")
         r.need("up_w", "down_w", "slope", "unit_one", "act", "normed_low")
@@ -1126,30 +1157,34 @@
             at_step(6 * (size - 1) + 14, ffn_below.to_chips),
             at_step(12 * (size - 1) + 6, ffn_below.onward),
         ]
+        extras += [
+            at_step(12 * (size - 1), lambda: r.need("proj_w_0")),
+            (12 * (size - 1), chunks, lambda chunk: context_back(below, chunk_rows(half, chunk))),
+        ]
         stages = [qkv_back_stage(above, 0, True), ffn_back_stage(middle, 0)]
         line_loop(size, stages, extras, 3)
-        r.need("proj_w_0", "qkv_w_0", "projected_0")
+        r.need("qkv_w_0", "projected_0")
         mixed_hop(1)
         attend_back(below)
         ffn_below.give_share()
         r.need("context_in_0", "low_in_0")
         extras = [
             *attn_grads(below, r.attn_whole_0, 0),
+            at_step(1, attn_below.to_partner),
             at_step(2, small_to_line),
-            *(at_step(4 + 6 * (hop - 2), lambda hop=hop: mixed_hop(hop)) for hop in range(2, end)),
-            at_step(7, small_to_teams),
-            at_step(15, small_finish),
-            at_step(1, attn_below.to_partner),
-            at_step(3, ffn_below.pass_on),
-            at_step(3, attn_below.to_chips),
-            at_step(9, ffn_below.to_other_core),
-            at_step(9, attn_below.onward),
-            at_step(11, lambda: (ffn_below.settle(), r.send("ffn_whole_0"))),
-            at_step(12, attn_below.give_share),
-            at_step(14, attn_below.pass_on),
-            at_step(18, attn_below.to_other_core),
+            at_step(4, ffn_below.pass_on),
+            at_step(4, attn_below.to_chips),
+            *(at_step(5 + 6 * (hop - 2), lambda hop=hop: mixed_hop(hop)) for hop in range(2, end)),
+            at_step(9, small_to_teams),
+            at_step(11, attn_below.onward),
+            at_step(12, ffn_below.to_other_core),
+            at_step(14, lambda: (ffn_below.settle(), r.send("ffn_whole_0"))),
+            at_step(15, attn_below.give_share),
+            at_step(18, attn_below.pass_on),
+            at_step(19, small_finish),
+            at_step(23, attn_below.to_other_core),
         ]
-        line_loop(size, [qkv_back_stage(below, 0, False)], extras)
+        line_loop(size, [qkv_back_stage(below, 0, False)], extras, 3)
         mixed_settle()
         r.send("grad_low", "mixed")
         attn_below.settle()
@@ -1208,7 +1243,7 @@
     layers = len(attn_wholes)
     rows, width = mixed.shape
     hidden = ffn_wholes[0].shape[0] - width
-    steps = 4
+    steps = 2
     cut = width // steps
 
     def for_layer(number, spec_of):

time: 322 us -> 319 us (level)
  no operation moved by 1% of the time
where the time goes in v2:
time: 319 us
  Pallas kernels  318 us (100%)
    pallas_call x2, Pallas kernels, call(): pl.pallas_call(run, out_shape=list(outs.values()), in_specs=[pl.BlockSpec...  303 us
    pallas_call x1, Pallas kernels, assemble(): pl.pallas_call(body, grid=(layers, steps), out_shape=out_shape, in_specs=...  14.5 us

profile of v2, /device:TPU:0, one launch (start us, length us, event | category | flops | bytes accessed | tf_op | source)
XLA Modules:
  0.0 318.6 jit_solution(8831941204126357820)
XLA Ops:
  0.6 167.5 %shard_map.254 = (bf16[3,512,256]{2,1,0:T(8,128)(2,1)}, f32[4,512]{1,0:T(4,128)}, bf16[512,256]{1,0:T(8,128)(2,1)}, bf16[3,512,256]{2,1,0:T(8,128)(2,1)}, f32[4,...) custom-call(bf16[512,1024]{1,0:T(8,128)(2,1)} %bitcast.22, ...), custom_call_target="tpu_custom_call" | custom-call | tf_op jit(solution)/shard_map/pallas_call | solution.py:565
  168.1 135.8 %shard_map.255 = (bf16[512,1024]{1,0:T(8,128)(2,1)}, bf16[512,1024]{1,0:T(8,128)(2,1)}, bf16[2048,1024]{1,0:T(8,128)(2,1)}, bf16[4096,256]{1,0:T(8,128)(2,1)}, b...) custom-call(s32[1,512]{1,0:T(1,128)} %refs_0_.1, f32[4,512]{1,0:T(4,128)} %get-tuple-element.55.refs_1_, ...), custom_call_target="tpu_custom_call" | custom-call | tf_op jit(solution)/shard_map/pallas_call | solution.py:565
  303.9 14.5 %shard_map.256 = (f32[512,1024]{1,0:T(8,128)}, f32[512,1024]{1,0:T(8,128)}, f32[2,3,1024,256]{3,2,1,0:T(8,128)}, f32[2,256,1024]{2,1,0:T(8,128)}, f32[2,1024,102...) custom-call(bf16[4,1024,256]{2,1,0:T(8,128)(2,1)} %bitcast.18, ...), custom_call_target="tpu_custom_call" | custom-call | tf_op jit(solution)/shard_map/pallas_call | solution.py:1325

commit v3 on v2

--- a/solution.py
+++ b/solution.py
@@ -139,24 +139,27 @@
                     def _():
                         row_copy(stage, which, side, chunk, back).start()
 
+    def begin_sum(stage, since):
+        for side in range(2):
+            at, onward, back = side_facts(side)
+
+            @pl.when(at == 0)
+            def _():
+                sum_copy(stage, side, since, onward).start()
+
     def sum_up(stage, since):
         for side in range(2):
             at, onward, back = side_facts(side)
             chunk = since - lag * at
 
-            @pl.when((chunk >= 0) & (chunk < chunks))
+            @pl.when((at > 0) & (chunk >= 0) & (chunk < chunks))
             def _():
-                @pl.when(at > 0)
-                def _():
-                    sum_copy(stage, side, chunk, onward).wait_recv()
+                sum_copy(stage, side, chunk, onward).wait_recv()
 
                 @pl.when(at < end)
                 def _():
-                    @pl.when(at > 0)
-                    def _():
-                        rows = rows_of(side, chunk)
-                        stage.part[rows] = stage.part[rows] + stage.recv[rows]
-
+                    rows = rows_of(side, chunk)
+                    stage.part[rows] = stage.part[rows] + stage.recv[rows]
                     sum_copy(stage, side, chunk, onward).start()
 
                 @pl.when(at == end)
@@ -172,13 +175,15 @@
         for number, stage in enumerate(stages):
             bring_back(stage, now - number * span)
         for number, stage in enumerate(stages):
+            sum_up(stage, now - number * span)
+        for number, stage in enumerate(stages):
             since = now - number * span
 
             @pl.when((since >= 0) & (since < chunks))
             def _():
                 stage.produce([rows_of(side, since) for side in range(2)])
-
-            sum_up(stage, since)
+                begin_sum(stage, since)
+
         for first, count, work in extras:
 
             @pl.when((now >= first) & (now < first + count))

time: 319 us -> 317 us (level)
  no operation moved by 1% of the time
where the time goes in v3:
time: 317 us
  Pallas kernels  316 us (100%)
    pallas_call x2, Pallas kernels, call(): pl.pallas_call(run, out_shape=list(outs.values()), in_specs=[pl.BlockSpec...  302 us
    pallas_call x1, Pallas kernels, assemble(): pl.pallas_call(body, grid=(layers, steps), out_shape=out_shape, in_specs=...  14.5 us

profile of v3, /device:TPU:0, one launch (start us, length us, event | category | flops | bytes accessed | tf_op | source)
XLA Modules:
  0.0 316.9 jit_solution(7856275224318111816)
XLA Ops:
  0.6 165.0 %shard_map.254 = (bf16[3,512,256]{2,1,0:T(8,128)(2,1)}, f32[4,512]{1,0:T(4,128)}, bf16[512,256]{1,0:T(8,128)(2,1)}, bf16[3,512,256]{2,1,0:T(8,128)(2,1)}, f32[4,...) custom-call(bf16[512,1024]{1,0:T(8,128)(2,1)} %bitcast.22, ...), custom_call_target="tpu_custom_call" | custom-call | tf_op jit(solution)/shard_map/pallas_call | solution.py:570
  165.6 136.6 %shard_map.255 = (bf16[512,1024]{1,0:T(8,128)(2,1)}, bf16[512,1024]{1,0:T(8,128)(2,1)}, bf16[2048,1024]{1,0:T(8,128)(2,1)}, bf16[4096,256]{1,0:T(8,128)(2,1)}, b...) custom-call(s32[1,512]{1,0:T(1,128)} %refs_0_.1, f32[4,512]{1,0:T(4,128)} %get-tuple-element.55.refs_1_, ...), custom_call_target="tpu_custom_call" | custom-call | tf_op jit(solution)/shard_map/pallas_call | solution.py:570
  302.3 14.5 %shard_map.256 = (f32[512,1024]{1,0:T(8,128)}, f32[512,1024]{1,0:T(8,128)}, f32[2,3,1024,256]{3,2,1,0:T(8,128)}, f32[2,256,1024]{2,1,0:T(8,128)}, f32[2,1024,102...) custom-call(bf16[4,1024,256]{2,1,0:T(8,128)(2,1)} %bitcast.18, ...), custom_call_target="tpu_custom_call" | custom-call | tf_op jit(solution)/shard_map/pallas_call | solution.py:1330

commit v4 on v3

--- a/solution.py
+++ b/solution.py
@@ -1181,13 +1181,13 @@
             at_step(4, attn_below.to_chips),
             *(at_step(5 + 6 * (hop - 2), lambda hop=hop: mixed_hop(hop)) for hop in range(2, end)),
             at_step(9, small_to_teams),
-            at_step(11, attn_below.onward),
+            at_step(10, attn_below.onward),
             at_step(12, ffn_below.to_other_core),
             at_step(14, lambda: (ffn_below.settle(), r.send("ffn_whole_0"))),
-            at_step(15, attn_below.give_share),
-            at_step(18, attn_below.pass_on),
+            at_step(13, attn_below.give_share),
+            at_step(16, attn_below.pass_on),
             at_step(19, small_finish),
-            at_step(23, attn_below.to_other_core),
+            at_step(21, attn_below.to_other_core),
         ]
         line_loop(size, [qkv_back_stage(below, 0, False)], extras, 3)
         mixed_settle()

time: 317 us -> 319 us (level)
  no operation moved by 1% of the time
where the time goes in v4:
time: 319 us
  Pallas kernels  318 us (100%)
    pallas_call x2, Pallas kernels, call(): pl.pallas_call(run, out_shape=list(outs.values()), in_specs=[pl.BlockSpec...  304 us
    pallas_call x1, Pallas kernels, assemble(): pl.pallas_call(body, grid=(layers, steps), out_shape=out_shape, in_specs=...  14.5 us

profile of v4, /device:TPU:0, one launch (start us, length us, event | category | flops | bytes accessed | tf_op | source)
XLA Modules:
  0.0 319.0 jit_solution(2604992854649584610)
XLA Ops:
  0.6 165.0 %shard_map.254 = (bf16[3,512,256]{2,1,0:T(8,128)(2,1)}, f32[4,512]{1,0:T(4,128)}, bf16[512,256]{1,0:T(8,128)(2,1)}, bf16[3,512,256]{2,1,0:T(8,128)(2,1)}, f32[4,...) custom-call(bf16[512,1024]{1,0:T(8,128)(2,1)} %bitcast.22, ...), custom_call_target="tpu_custom_call" | custom-call | tf_op jit(solution)/shard_map/pallas_call | solution.py:570
  165.6 138.7 %shard_map.255 = (bf16[512,1024]{1,0:T(8,128)(2,1)}, bf16[512,1024]{1,0:T(8,128)(2,1)}, bf16[2048,1024]{1,0:T(8,128)(2,1)}, bf16[4096,256]{1,0:T(8,128)(2,1)}, b...) custom-call(s32[1,512]{1,0:T(1,128)} %refs_0_.1, f32[4,512]{1,0:T(4,128)} %get-tuple-element.55.refs_1_, ...), custom_call_target="tpu_custom_call" | custom-call | tf_op jit(solution)/shard_map/pallas_call | solution.py:570
  304.3 14.5 %shard_map.256 = (f32[512,1024]{1,0:T(8,128)}, f32[512,1024]{1,0:T(8,128)}, f32[2,3,1024,256]{3,2,1,0:T(8,128)}, f32[2,256,1024]{2,1,0:T(8,128)}, f32[2,1024,102...) custom-call(bf16[4,1024,256]{2,1,0:T(8,128)(2,1)} %bitcast.18, ...), custom_call_target="tpu_custom_call" | custom-call | tf_op jit(solution)/shard_map/pallas_call | solution.py:1330
